TPU v7x, 32 devices: a whole 2x2x4 slice. The times are simulated.
32 devices in a mesh: ia: 2 (over y), ib: 4 (over z), op: 4 (over x, core).
Axes of the slice: x: 2, y: 2, z: 4, core: 2. Of those that a mesh axis runs over, the one named last changes fastest.
Arguments:
- fit_coefficients: bfloat16 [2, 3072, 4096], P('ia', ('ib', 'op')), may hold values from -0.09375 to 0.09375
- three_center: bfloat16 [2, 4096, 3072], P(None, None, ('ib', 'op')), may hold values from -6 to 6
- amplitudes: bfloat16 [32, 3072, 3072], P('op', ('ia', 'ib')), may hold values from -0.001953125 to 0.001953125
- pair_list: int32 [32, 2], P('op'), may hold values from 0 to 255
- slot_tiles: int32 [8], replicated, may hold values from 0 to 7, each once
- energy_occupied: float32 [256], replicated, may hold values from -1.2 to -0.4
- energy_left: float32 [2], P('ia'), may hold values from 0.3 to 2.5
- energy_right: float32 [2], replicated, may hold values from 0.3 to 2.5
Outputs:
- update: float32 [32, 2, 2], P('op', 'ia')
Inputs may be any that keep to these rules, and one draw needn't show every extreme that they name: `slot_tiles`: each tile number stands in exactly one slot.
All inputs are finite; a program needn't handle non-finite values.
Results may differ from a plain program's by a relative error of at most 0.0029.
Values may be sent and summed in bfloat16 or wider, within the bound.
A program may use at most 128 MiB of HBM per device.

v0:
```python
import jax
import jax.numpy as jnp
from jax import lax
from jax.sharding import PartitionSpec as P

laplace_points = (0.06, 0.25, 0.7, 1.6, 3.5)
laplace_weights = (0.16, 0.36, 0.62, 1.0, 1.7)


def per_device(
    fit_coefficients,
    three_center,
    amplitudes,
    pair_list,
    slot_tiles,
    energy_occupied,
    energy_left,
    energy_right,
):
    left_rows = fit_coefficients.shape[0]
    right_rows = three_center.shape[0]
    share = three_center.shape[2]
    tile_width = amplitudes.shape[1]
    local_pairs = amplitudes.shape[0]
    left_count = lax.axis_size("ia")
    right_count = lax.axis_size("ib")
    group_count = lax.axis_size("op")
    slot_count = left_count * right_count
    integral_tiles = jnp.einsum(
        "oiu,tup->otip",
        lax.all_gather(fit_coefficients, ("ib", "op"), axis=1, tiled=True),
        three_center,
        preferred_element_type=jnp.float32,
    ).astype(jnp.bfloat16)
    ordered = jnp.take(
        integral_tiles.reshape(left_rows, right_rows, slot_count, tile_width, share),
        slot_tiles,
        axis=2,
    )
    arrived = lax.all_to_all(ordered, ("ia", "ib"), split_axis=2, concat_axis=0, tiled=True)
    received = arrived.reshape(left_count, right_count, right_rows, tile_width, share)
    split_amps = amplitudes.reshape(local_pairs, tile_width, right_count, group_count * share)
    partial_value = jnp.einsum(
        "pkie,aibke->pab",
        split_amps,
        lax.all_gather(received, "op", axis=4, tiled=True),
        preferred_element_type=jnp.float32,
    )
    summed = lax.psum(partial_value, ("ia", "ib"))
    owned = lax.dynamic_slice(summed, (0, lax.axis_index("ia"), 0), (local_pairs, 1, right_rows))
    occupied = energy_occupied.shape[0]
    column = lax.broadcasted_iota(jnp.int32, (local_pairs, occupied), 1)
    occupied_one = jnp.sum(
        jnp.where(pair_list[:, 0:1] == column, energy_occupied[None, :], 0.0), axis=1
    )
    occupied_two = jnp.sum(
        jnp.where(pair_list[:, 1:2] == column, energy_occupied[None, :], 0.0), axis=1
    )
    occupied_sum = occupied_one + occupied_two
    denominator = (
        energy_left[None, :, None] + energy_right[None, None, :] - occupied_sum[:, None, None]
    )
    factor = jnp.zeros_like(denominator)
    for point, weight in zip(laplace_points, laplace_weights):
        factor = factor + weight * jnp.exp(-point * denominator)
    return owned * factor


def solution(mesh):
    placed = (
        P("ia", ("ib", "op"), None),
        P(None, None, ("ib", "op")),
        P("op", ("ia", "ib"), None),
        P("op", None),
        P(),
        P(),
        P("ia"),
        P(),
    )
    return jax.shard_map(
        per_device, mesh=mesh, in_specs=placed, out_specs=P("op", "ia", None), check_vma=False
    )
```

profile of v0, /device:TPU:0, one launch (start us, length us, event | category | flops | bytes accessed | tf_op | source)
XLA Modules:
  0.0 357.5 jit_solution(4936656628744574607)
XLA Ops:
  6.5 0.0 copy-start
  6.5 0.0 all-gather.3.cloned.1.call-start
  6.5 0.7 all-gather.3.cloned.1.call-update
  7.3 0.0 all-gather.5.cloned.1.call-start
  7.3 0.8 compare_select_fusion
  8.1 0.7 compare_and_fusion
  8.8 131.5 %all-gather.3.cloned.1.call-done = bf16[1,3072,4096]{2,1,0:T(8,128)(2,1)} async-done(((bf16[1,192,4096]{2,1,0:T(8,128)(2,1)}), bf16[1,3072,4096]{2,1,0:T(8,128)(2,1)}) %all-gather.3.cloned.1.call-update) | async-done | bytes 25165840 | tf_op jit(solution)/shard_map/all_gather | solution.py:31
  140.3 0.0 copy-done
  140.3 15.3 %fusion.5 = bf16[2,192,3072]{2,1,0:T(8,128)(2,1)} fusion(bf16[2,4096,192]{1,2,0:T(8,128)(2,1)S(1)} %copy-done, bf16[1,3072,4096]{2,1,0:T(8,128)(2,1)} %all-gather.3.cloned.1.call-done), kind=kOutput, calls=%fused_computation.6 | convolution fusion | flops 9664856064 | bytes 30670848 | tf_op jit(solution)/shard_map/oiu,tup->otip/dot_general | solution.py:29
  155.6 2.2 copy.28
  157.8 1.8 copy.22
  159.6 2.7 gather_fusion
  162.3 0.3 fusion.8
  162.7 60.4 %all_to_all.15 = bf16[1,2,8,384,192]{3,4,1,0,2:T(8,128)(2,1)S(1)} all-to-all(bf16[1,2,8,384,192]{3,4,1,0,2:T(8,128)(2,1)S(1)} %fusion.8), channel_id=1, replica_groups=mesh['ia'=2,'ib'=4,'op'=4] {'ia','ib'}, dimensions={2} | all-to-all | bytes 4718592 | tf_op jit(solution)/shard_map/all_to_all | solution.py:40
  223.1 3.2 copy.24
  226.3 0.0 all-gather.5.cloned.1.call-update
  226.3 35.1 %reshape.158 = bf16[8,384,4,768]{3,2,1,0:T(4,128)(2,1)} reshape(bf16[8,384,3072]{2,1,0:T(8,128)(2,1)} %param.10) | data formatting | bytes 37748736 | tf_op jit(solution)/shard_map/reshape | solution.py:42
  261.4 0.0 copy-start.3
  261.4 0.0 copy-start.2
  261.4 0.0 copy-start.4
  261.4 32.6 %copy.26 = bf16[8,384,4,768]{1,0,2,3:T(8,128)(2,1)} copy(bf16[8,384,4,768]{3,2,1,0:T(4,128)(2,1)} %reshape.158) | data formatting | bytes 37748736 | tf_op jit(solution)/shard_map/reshape | solution.py:42
  294.7 0.0 copy-done.3
  294.7 0.0 copy-done.2
  294.7 0.2 select_reduce_fusion
  295.0 0.0 copy-done.4
  295.0 0.0 all-gather.5.cloned.1.call-done
  295.0 0.0 copy-start.1
  295.0 37.6 %fusion.9 = f32[8,2,2]{0,2,1:T(2,128)S(1)} fusion(bf16[8,384,4,768]{1,0,2,3:T(8,128)(2,1)} %copy.26, bf16[2,4,2,384,768]{3,1,2,0,4:T(4,128)(2,1)} %all-gather.5.cloned.1.call-done), kind=kOutput, calls=%fused_computation.9 | convolution fusion | flops 75497472 | bytes 28311680 | tf_op jit(solution)/shard_map/pkie,aibke->pab/dot_general | solution.py:43
  332.6 17.4 %psum.7 = f32[8,2,2]{0,2,1:T(2,128)S(1)} all-reduce(f32[8,2,2]{0,2,1:T(2,128)S(1)} %fusion.9), channel_id=1, replica_groups=mesh['ia'=2,'ib'=4,'op'=4] {'ia','ib'}, use_global_device_ids=true, to_apply=%region_0.1 | all-reduce | flops 32 | bytes 256 | tf_op jit(solution)/shard_map/psum | solution.py:49
  350.0 0.6 fusion.24
  350.7 0.0 copy-done.1
  (4 shorter events, 0.0 us)
Async XLA Ops:
  6.5 133.7 %copy-start = (bf16[2,4096,192]{1,2,0:T(8,128)(2,1)S(1)}, bf16[2,4096,192]{1,2,0:T(8,128)(2,1)}, u32[]{:S(2)}) copy-start(bf16[2,4096,192]{1,2,0:T(8,128)(2,1)} %param.9) | copy-start | bytes 9437188
  6.5 133.7 %all-gather.3.cloned.1.call-start = ((), (), s32[]{:S(2)}) async-start(), calls=%async_computation.1 | async-start | bytes 26738688 | tf_op jit(solution)/shard_map/all_gather | solution.py:31
  7.3 287.7 %all-gather.5.cloned.1.call-start = ((), (), s32[]{:S(2)}) async-start(), calls=%async_computation.2 | async-start | bytes 11796480 | tf_op jit(solution)/shard_map/all_gather | solution.py:46
  261.4 33.3 %copy-start.3 = (s32[8,2]{0,1:T(2,128)S(1)}, s32[8,2]{0,1:T(2,128)}, u32[]{:S(2)}) copy-start(s32[8,2]{0,1:T(2,128)} %param.11) | copy-start | bytes 196
  261.4 33.3 %copy-start.2 = (f32[256]{0:T(256)S(1)}, f32[256]{0:T(256)}, u32[]{:S(2)}) copy-start(f32[256]{0:T(256)} %param.13) | copy-start | bytes 3076
  261.4 33.5 %copy-start.4 = (f32[2]{0:T(128)S(1)}, f32[2]{0:T(128)}, u32[]{:S(2)}) copy-start(f32[2]{0:T(128)} %param.15) | copy-start | bytes 28
  295.0 55.7 %copy-start.1 = (bf16[2,4096,192]{1,2,0:T(8,128)(2,1)S(1)}, bf16[2,4096,192]{1,2,0:T(8,128)(2,1)}, u32[]{:S(2)}) copy-start(bf16[2,4096,192]{1,2,0:T(8,128)(2,1)} %param.9) | copy-start | bytes 9437188
Sparse Core Ops, SparseCore 0:
  9.0 131.2 all-gather.2
  226.4 60.5 all-gather.4
where the time goes:
time: 359 us; the launch traced here: 358 us
  waiting for transfers between devices  132 us (37%)
  blocking collectives  77.8 us (22%)
  local copies, waits for them, and re-layouts  77.7 us (22%)
  matrix products  52.9 us (15%)
  between operations  14.2 us (4%)
    all_gather x1, waiting for transfers between devices, per_device(): lax.all_gather(fit_coefficients, ('ib', 'op'), axis=1, tiled=True)  131 us
    reshape x2, local copies, waits for them, and re-layouts, per_device(): amplitudes.reshape(local_pairs, tile_width, right_count, group_count * sh...  67.7 us
    all_to_all x1, blocking collectives, per_device(): lax.all_to_all(ordered, ('ia', 'ib'), split_axis=2, concat_axis=0, tiled=...  60.4 us
    dot_general x1, matrix products, per_device(): jnp.einsum('pkie,aibke->pab', split_amps, lax.all_gather(received, 'op',...  37.6 us
    psum x1, blocking collectives, per_device(): summed = lax.psum(partial_value, ('ia', 'ib'))  17.4 us
    dot_general x1, matrix products, per_device(): jnp.einsum('oiu,tup->otip', lax.all_gather(fit_coefficients, ('ib', 'op')...  15.3 us
  transfers between devices with their start and end apart: 2, of which 1 were waited for; matrix products, arithmetic and copies ran while one was open for 19% of the time, Pallas kernels for 0%

commit v1 on v0

v1 whole, which is shorter than its diff:
```python
import functools

import jax
import jax.numpy as jnp
from jax import lax
from jax.experimental import pallas as pl
from jax.experimental.pallas import tpu as pltpu
from jax.sharding import PartitionSpec as P

laplace_points = (0.06, 0.25, 0.7, 1.6, 3.5)
laplace_weights = (0.16, 0.36, 0.62, 1.0, 1.7)
lanes = 128


def tiles_kernel(slots_ref, *refs):
    *coefficient_refs, center_ref, out_ref = refs
    rows = jnp.concatenate([r[0] for r in coefficient_refs], axis=0)
    product = lax.dot_general(
        center_ref[...], rows, (((1,), (1,)), ((), ())), preferred_element_type=jnp.float32
    ).astype(jnp.bfloat16)
    for i in range(len(coefficient_refs)):
        out_ref[i] = product[:, i * lanes : (i + 1) * lanes]


def integral_tiles(coefficients, center, slot_tiles, pair=2):
    slots, width, aux = coefficients.shape
    columns = center.shape[0]
    specs = [
        pl.BlockSpec((1, width, aux), lambda s, t, i=i: (t[s * pair + i], 0, 0)) for i in range(pair)
    ]
    return pl.pallas_call(
        tiles_kernel,
        out_shape=jax.ShapeDtypeStruct((slots, columns, width), jnp.bfloat16),
        grid_spec=pltpu.PrefetchScalarGridSpec(
            num_scalar_prefetch=1,
            grid=(slots // pair,),
            in_specs=[*specs, pl.BlockSpec((columns, aux), lambda s, t: (0, 0))],
            out_specs=pl.BlockSpec((pair, columns, width), lambda s, t: (s, 0, 0)),
        ),
        compiler_params=pltpu.CompilerParams(vmem_limit_bytes=40 * 2**20),
        cost_estimate=pl.CostEstimate(
            flops=2 * slots * columns * width * aux,
            bytes_accessed=2 * (slots * width * aux + columns * aux + slots * columns * width),
            transcendentals=0,
        ),
    )(slot_tiles, *([coefficients] * pair), center)


def contract_kernel(amps_ref, tiles_ref, out_ref, total):
    step = pl.program_id(0) * pl.num_programs(1) + pl.program_id(1)
    steps = pl.num_programs(0) * pl.num_programs(1)
    pairs, halves, rows, depth = amps_ref.shape
    left = amps_ref[...].reshape(pairs * halves * rows, depth)
    _, merged, a_count, _, b_count, share, width = tiles_ref.shape
    right = jnp.concatenate(
        [
            jnp.concatenate([tiles_ref[0, m, a, 0, b] for m in range(merged)], axis=0)
            for a in range(a_count)
            for b in range(b_count)
        ],
        axis=1,
    )
    product = jnp.dot(left, right, preferred_element_type=jnp.float32)

    @pl.when(step == 0)
    def _():
        total[...] = product

    @pl.when(step > 0)
    def _():
        total[...] += product

    @pl.when(step == steps - 1)
    def _():
        count = total.shape[1]
        row = lax.broadcasted_iota(jnp.int32, (halves * rows, count), 0)
        column = lax.broadcasted_iota(jnp.int32, (halves * rows, count), 1) % width
        kept = row == column
        for p in range(pairs):
            block = total[p * halves * rows : (p + 1) * halves * rows, :]
            out_ref[p : p + 1, :] = jnp.sum(jnp.where(kept, block, 0.0), axis=0, keepdims=True)


def contract(amps, tiles, chunk):
    pairs, halves, _, _ = amps.shape
    groups, merged, a_count, ib_count, b_count, share, width = tiles.shape
    rows = width // halves
    depth = merged * share
    columns = a_count * b_count * width
    return pl.pallas_call(
        contract_kernel,
        out_shape=jax.ShapeDtypeStruct((pairs, columns), jnp.float32),
        grid=(ib_count, groups),
        in_specs=[
            pl.BlockSpec((pairs, halves, rows, depth), lambda i, g: (0, 0, chunk, i * groups + g)),
            pl.BlockSpec(
                (1, merged, a_count, 1, b_count, share, width), lambda i, g: (g, 0, 0, i, 0, 0, 0)
            ),
        ],
        out_specs=pl.BlockSpec((pairs, columns), lambda i, g: (0, 0)),
        scratch_shapes=[pltpu.VMEM((pairs * halves * rows, columns), jnp.float32)],
        compiler_params=pltpu.CompilerParams(vmem_limit_bytes=40 * 2**20),
        cost_estimate=pl.CostEstimate(
            flops=2 * pairs * width * columns * depth * ib_count * groups,
            bytes_accessed=2 * (pairs * width * depth * ib_count * groups + tiles.size),
            transcendentals=0,
        ),
    )(amps, tiles)


def chunked(fit_coefficients, three_center, amplitudes, slot_tiles):
    left_rows, own_rows, aux = fit_coefficients.shape
    right_rows, _, share = three_center.shape
    local_pairs, tile_width, full = amplitudes.shape
    left_count, right_count = lax.axis_size("ia"), lax.axis_size("ib")
    group_count = lax.axis_size("op")
    slots = left_count * right_count
    halves = tile_width // own_rows
    rows = lanes // halves
    center = jnp.transpose(three_center, (0, 2, 1)).reshape(right_rows * share, aux)
    amps = amplitudes.reshape(local_pairs, halves, own_rows, full)
    value = 0.0
    for j in range(own_rows // rows):
        piece = lax.all_gather(
            fit_coefficients[0, j * rows : (j + 1) * rows], ("ib", "op"), axis=0, tiled=True
        )
        tiles = integral_tiles(piece.reshape(slots, lanes, aux), center, slot_tiles)
        arrived = lax.all_to_all(tiles, ("ia", "ib"), split_axis=0, concat_axis=0, tiled=True)
        spread = lax.all_gather(arrived, "op", axis=0, tiled=True)
        spread = spread.reshape(
            group_count // 2, 2, left_count, right_count, right_rows, share, lanes
        )
        value = value + contract(amps, spread, j)
    return value.reshape(local_pairs, left_count, right_rows, lanes).sum(axis=3)


def whole_at_once(fit_coefficients, three_center, amplitudes, slot_tiles):
    left_rows = fit_coefficients.shape[0]
    right_rows = three_center.shape[0]
    share = three_center.shape[2]
    tile_width = amplitudes.shape[1]
    local_pairs = amplitudes.shape[0]
    left_count, right_count = lax.axis_size("ia"), lax.axis_size("ib")
    group_count = lax.axis_size("op")
    slot_count = left_count * right_count
    tiles = jnp.einsum(
        "oiu,tup->otip",
        lax.all_gather(fit_coefficients, ("ib", "op"), axis=1, tiled=True),
        three_center,
        preferred_element_type=jnp.float32,
    ).astype(jnp.bfloat16)
    tiles = tiles.reshape(left_rows, right_rows, slot_count, tile_width, share)
    ordered = jnp.concatenate(
        [lax.dynamic_slice_in_dim(tiles, slot_tiles[s], 1, axis=2) for s in range(slot_count)],
        axis=2,
    )
    arrived = lax.all_to_all(ordered, ("ia", "ib"), split_axis=2, concat_axis=0, tiled=True)
    received = arrived.reshape(left_count, right_count, left_rows, right_rows, tile_width, share)
    split_amps = amplitudes.reshape(local_pairs, tile_width, right_count, group_count * share)
    value = jnp.einsum(
        "pkie,aiobke->paob",
        split_amps,
        lax.all_gather(received, "op", axis=5, tiled=True),
        preferred_element_type=jnp.float32,
    )
    return value.reshape(local_pairs, left_count * left_rows, right_rows)


def per_device(
    fit_coefficients,
    three_center,
    amplitudes,
    pair_list,
    slot_tiles,
    energy_occupied,
    energy_left,
    energy_right,
):
    left_rows, own_rows, _ = fit_coefficients.shape
    right_rows, _, share = three_center.shape
    local_pairs, tile_width, _ = amplitudes.shape
    halves = tile_width // own_rows
    fits = (
        left_rows == 1
        and halves > 0
        and tile_width == halves * own_rows
        and lanes % max(halves, 1) == 0
        and own_rows % (lanes // max(halves, 1)) == 0
        and (lanes // max(halves, 1)) % 16 == 0
        and lax.axis_size("op") % 2 == 0
        and (2 * share) % lanes == 0
        and share % 16 == 0
        and (lax.axis_size("ia") * lax.axis_size("ib")) % 2 == 0
    )
    partial_value = (chunked if fits else whole_at_once)(
        fit_coefficients, three_center, amplitudes, slot_tiles
    )
    summed = lax.psum(partial_value, ("ia", "ib"))
    owned = lax.dynamic_slice(
        summed,
        (0, lax.axis_index("ia") * left_rows, 0),
        (local_pairs, left_rows, right_rows),
    )
    occupied = energy_occupied.shape[0]
    column = lax.broadcasted_iota(jnp.int32, (local_pairs, occupied), 1)
    occupied_one = jnp.sum(
        jnp.where(pair_list[:, 0:1] == column, energy_occupied[None, :], 0.0), axis=1
    )
    occupied_two = jnp.sum(
        jnp.where(pair_list[:, 1:2] == column, energy_occupied[None, :], 0.0), axis=1
    )
    occupied_sum = occupied_one + occupied_two
    denominator = (
        energy_left[None, :, None] + energy_right[None, None, :] - occupied_sum[:, None, None]
    )
    factor = jnp.zeros_like(denominator)
    for point, weight in zip(laplace_points, laplace_weights):
        factor = factor + weight * jnp.exp(-point * denominator)
    return owned * factor


def solution(mesh):
    placed = (
        P("ia", ("ib", "op"), None),
        P(None, None, ("ib", "op")),
        P("op", ("ia", "ib"), None),
        P("op", None),
        P(),
        P(),
        P("ia"),
        P(),
    )
    return jax.shard_map(
        per_device, mesh=mesh, in_specs=placed, out_specs=P("op", "ia", None), check_vma=False
    )
```

time: 359 us -> 399 us (1.11)
  waiting for transfers between devices: 132 us -> 196 us
  local copies, waits for them, and re-layouts: 77.7 us -> 18.8 us
  matrix products: 52.9 us -> 0 us
  blocking collectives: 77.8 us -> 125 us
  Pallas kernels: 0 us -> 43 us
    reshape x4 -> x0, local copies, waits for them, and re-layouts: 72.7 us -> none  [the longest x2 67.7 us: per_device(): amplitudes.reshape(local_pairs, tile_width, right_count, group_count * sh...]
    all_gather x2 -> x6, waiting for transfers between devices: 131 us -> 195 us  [the longest x3 164 us: chunked(): lax.all_gather(fit_coefficients[0, j * rows:(j + 1) * rows], ('ib', 'op')...]
    dot_general x2 -> x0, matrix products: 52.9 us -> none  [the longest x1 37.6 us: per_device(): jnp.einsum('pkie,aibke->pab', split_amps, lax.all_gather(received, 'op',...]
    all_to_all x1 -> x3, blocking collectives: 60.4 us -> 104 us  [chunked(): lax.all_to_all(tiles, ('ia', 'ib'), split_axis=0, concat_axis=0, tiled=True)]
    pallas_call x0 -> x6, Pallas kernels: none -> 43 us  [the longest x3 29.1 us: contract(): pl.pallas_call(contract_kernel, out_shape=jax.ShapeDtypeStruct((pairs, co...]
    unnamed x11 -> x22, local copies, waits for them, and re-layouts: 2.19 us -> 16 us
    psum x1, blocking collectives: 17.4 us -> 21.4 us  [per_device(): summed = lax.psum(partial_value, ('ia', 'ib'))]
  transfers between devices with their start and end apart: 2 -> 6, of which waited for: 1 -> 5; matrix products, arithmetic and copies ran while one was open for 19% -> 0% of each run, Pallas kernels for 0% -> 8%
where the time goes in v1:
time: 399 us; the launch traced here: 398 us
  waiting for transfers between devices  196 us (49%)
  blocking collectives  125 us (31%)
  Pallas kernels  43 us (11%)
  local copies, waits for them, and re-layouts  18.8 us (5%)
  between operations  14.2 us (4%)
    all_gather x3, waiting for transfers between devices, chunked(): lax.all_gather(fit_coefficients[0, j * rows:(j + 1) * rows], ('ib', 'op')...  164 us
    all_to_all x3, blocking collectives, chunked(): lax.all_to_all(tiles, ('ia', 'ib'), split_axis=0, concat_axis=0, tiled=True)  104 us
    all_gather x3, waiting for transfers between devices, chunked(): spread = lax.all_gather(arrived, 'op', axis=0, tiled=True)  30.6 us
    pallas_call x3, Pallas kernels, contract(): pl.pallas_call(contract_kernel, out_shape=jax.ShapeDtypeStruct((pairs, co...  29.1 us
    psum x1, blocking collectives, per_device(): summed = lax.psum(partial_value, ('ia', 'ib'))  21.4 us
    unnamed x22, local copies, waits for them, and re-layouts  16 us
    pallas_call x3, Pallas kernels, integral_tiles(): pl.pallas_call(tiles_kernel, out_shape=jax.ShapeDtypeStruct((slots, colum...  13.9 us
  transfers between devices with their start and end apart: 6, of which 5 were waited for; matrix products, arithmetic and copies ran while one was open for 0% of the time, Pallas kernels for 8%

profile of v1, /device:TPU:0, one launch (start us, length us, event | category | flops | bytes accessed | tf_op | source)
XLA Modules:
  0.0 398.5 jit_solution(10491478016359343644)
XLA Ops:
  6.5 2.8 fusion.14
  9.4 0.0 all-gather.18.cloned.1.call-start
  9.4 0.7 all-gather.18.cloned.1.call-update
  10.1 0.0 all-gather.20.cloned.1.call-start
  10.2 0.7 all-gather.20.cloned.1.call-update
  10.9 0.0 all-gather.10.cloned.1.call-start
  10.9 76.2 %all-gather.16.cloned.1.call-done = bf16[1,1024,4096]{2,1,0:T(8,128)(2,1)} async-done(((bf16[1,64,4096]{2,1,0:T(8,128)(2,1)}), bf16[1,1024,4096]{2,1,0:T(8,128)(2,1)}) %all-gather.16.cloned.1.call-update) | async-done | bytes 8388624 | tf_op jit(solution)/shard_map/all_gather | solution.py:124
  87.2 3.4 copy-done.2
  90.5 4.6 %shard_map.82 = bf16[8,384,128]{2,1,0:T(8,128)(2,1)S(1)} custom-call(s32[8]{0:T(128)S(1)} %copy-done.7, bf16[8,128,4096]{2,1,0:T(8,128)(2,1)S(1)} %bitcast.21, bf16[8,128,4096]{2,1,0:T(8,128)(2,1)S(1)} %bitcast.22, bf16[384,4096]{1,0:T(8,128)(2,1)S(1)} %bitcast.23), custom_call_target="tpu_custom_call" | custom-call | flops 3221225472 | bytes 12320768 | tf_op jit(solution)/shard_map/pallas_call | solution.py:31
  95.2 39.3 %all_to_all.15 = bf16[8,384,128]{2,1,0:T(8,128)(2,1)} all-to-all(bf16[8,384,128]{2,1,0:T(8,128)(2,1)S(1)} %shard_map.82), channel_id=1, replica_groups=mesh['ia'=2,'ib'=4,'op'=4] {'ia','ib'}, dimensions={0} | all-to-all | bytes 1572864 | tf_op jit(solution)/shard_map/all_to_all | solution.py:128
  134.5 0.0 all-gather.12.cloned.1.call-start
  134.5 43.9 %all-gather.18.cloned.1.call-done = bf16[1,1024,4096]{2,1,0:T(8,128)(2,1)} async-done(((bf16[1,64,4096]{2,1,0:T(8,128)(2,1)}), bf16[1,1024,4096]{2,1,0:T(8,128)(2,1)}) %all-gather.18.cloned.1.call-update) | async-done | bytes 8388624 | tf_op jit(solution)/shard_map/all_gather | solution.py:124
  178.5 3.4 copy-done.1
  181.8 4.6 %shard_map.84 = bf16[8,384,128]{2,1,0:T(8,128)(2,1)S(1)} custom-call(s32[8]{0:T(128)S(1)} %copy-done.7, bf16[8,128,4096]{2,1,0:T(8,128)(2,1)S(1)} %bitcast.19, bf16[8,128,4096]{2,1,0:T(8,128)(2,1)S(1)} %bitcast.20, bf16[384,4096]{1,0:T(8,128)(2,1)S(1)} %bitcast.24), custom_call_target="tpu_custom_call" | custom-call | flops 3221225472 | bytes 12320768 | tf_op jit(solution)/shard_map/pallas_call | solution.py:31
  186.5 39.3 %all_to_all.16 = bf16[8,384,128]{2,1,0:T(8,128)(2,1)} all-to-all(bf16[8,384,128]{2,1,0:T(8,128)(2,1)S(1)} %shard_map.84), channel_id=1, replica_groups=mesh['ia'=2,'ib'=4,'op'=4] {'ia','ib'}, dimensions={0} | all-to-all | bytes 1572864 | tf_op jit(solution)/shard_map/all_to_all | solution.py:128
  225.8 0.0 all-gather.14.cloned.1.call-start
  225.8 44.0 %all-gather.20.cloned.1.call-done = bf16[1,1024,4096]{2,1,0:T(8,128)(2,1)} async-done(((bf16[1,64,4096]{2,1,0:T(8,128)(2,1)}), bf16[1,1024,4096]{2,1,0:T(8,128)(2,1)}) %all-gather.20.cloned.1.call-update) | async-done | bytes 8388624 | tf_op jit(solution)/shard_map/all_gather | solution.py:124
  269.8 3.4 copy-done
  273.2 4.6 %shard_map.86 = bf16[8,384,128]{2,1,0:T(8,128)(2,1)S(1)} custom-call(s32[8]{0:T(128)S(1)} %copy-done.7, bf16[8,128,4096]{2,1,0:T(8,128)(2,1)S(1)} %bitcast.17, bf16[8,128,4096]{2,1,0:T(8,128)(2,1)S(1)} %bitcast.18, bf16[384,4096]{1,0:T(8,128)(2,1)S(1)} %bitcast.25), custom_call_target="tpu_custom_call" | custom-call | flops 3221225472 | bytes 12320768 | tf_op jit(solution)/shard_map/pallas_call | solution.py:31
  277.8 25.1 %all_to_all.17 = bf16[8,384,128]{2,1,0:T(8,128)(2,1)} all-to-all(bf16[8,384,128]{2,1,0:T(8,128)(2,1)S(1)} %shard_map.86), channel_id=1, replica_groups=mesh['ia'=2,'ib'=4,'op'=4] {'ia','ib'}, dimensions={0} | all-to-all | bytes 1572864 | tf_op jit(solution)/shard_map/all_to_all | solution.py:128
  303.6 0.2 select_reduce_fusion
  303.9 2.0 copy-done.4
  305.9 9.7 %shard_map.83 = f32[8,512]{1,0:T(8,128)S(1)} custom-call(bf16[8,2,192,3072]{3,2,1,0:T(8,128)(2,1)} %bitcast.29, bf16[2,2,2,4,2,192,128]{6,5,4,3,2,1,0:T(8,128)(2,1)S(1)} %bitcast.26), custom_call_target="tpu_custom_call" | custom-call | flops 3221225472 | bytes 9437184 | tf_op jit(solution)/shard_map/pallas_call | solution.py:90
  315.6 12.4 %all-gather.12.cloned.1.call-done = bf16[32,384,128]{2,1,0:T(8,128)(2,1)} async-done(((bf16[8,384,128]{2,1,0:T(8,128)(2,1)}), bf16[32,384,128]{2,1,0:T(8,128)(2,1)}) %all-gather.12.cloned.1.call-update) | async-done | bytes 3145744 | tf_op jit(solution)/shard_map/all_gather | solution.py:129
  328.0 1.9 copy-done.5
  329.9 9.8 %shard_map.85 = f32[8,512]{1,0:T(8,128)S(1)} custom-call(bf16[8,2,192,3072]{3,2,1,0:T(8,128)(2,1)} %bitcast.30, bf16[2,2,2,4,2,192,128]{6,5,4,3,2,1,0:T(8,128)(2,1)S(1)} %bitcast.27), custom_call_target="tpu_custom_call" | custom-call | flops 3221225472 | bytes 9437184 | tf_op jit(solution)/shard_map/pallas_call | solution.py:90
  339.7 18.2 %all-gather.14.cloned.1.call-done = bf16[32,384,128]{2,1,0:T(8,128)(2,1)} async-done(((bf16[8,384,128]{2,1,0:T(8,128)(2,1)}), bf16[32,384,128]{2,1,0:T(8,128)(2,1)}) %all-gather.14.cloned.1.call-update) | async-done | bytes 3145744 | tf_op jit(solution)/shard_map/all_gather | solution.py:129
  358.0 1.9 copy-done.6
  359.9 9.6 %shard_map.87 = f32[8,512]{1,0:T(8,128)S(1)} custom-call(bf16[8,2,192,3072]{3,2,1,0:T(8,128)(2,1)} %bitcast.31, bf16[2,2,2,4,2,192,128]{6,5,4,3,2,1,0:T(8,128)(2,1)S(1)} %bitcast.28), custom_call_target="tpu_custom_call" | custom-call | flops 3221225472 | bytes 9437184 | tf_op jit(solution)/shard_map/pallas_call | solution.py:90
  369.4 0.1 reduce_sum.27
  369.5 21.4 %psum.7 = f32[8,2,2]{0,2,1:T(2,128)S(1)} all-reduce(f32[8,2,2]{0,2,1:T(2,128)S(1)} %reduce_sum.27), channel_id=1, replica_groups=mesh['ia'=2,'ib'=4,'op'=4] {'ia','ib'}, use_global_device_ids=true, to_apply=%region_1.0 | all-reduce | flops 32 | bytes 256 | tf_op jit(solution)/shard_map/psum | solution.py:198
  391.0 0.6 fusion.10
  (26 shorter events, 0.1 us)
Async XLA Ops:
  6.5 80.6 %copy-start.3 = (bf16[2,4096,192]{1,2,0:T(8,128)(2,1)S(1)}, bf16[2,4096,192]{1,2,0:T(8,128)(2,1)}, u32[]{:S(2)}) copy-start(bf16[2,4096,192]{1,2,0:T(8,128)(2,1)} %param.9) | copy-start | bytes 9437188
  6.5 80.6 %copy-start.7 = (s32[8]{0:T(128)S(1)}, s32[8]{0:T(128)}, u32[]{:S(2)}) copy-start(s32[8]{0:T(128)} %slots_ref.5) | copy-start | bytes 100
  6.5 80.6 %all-gather.16.cloned.1.call-start = ((), (), s32[]{:S(2)}) async-start(), calls=%async_computation.6 | async-start | bytes 8912896 | tf_op jit(solution)/shard_map/all_gather | solution.py:124
  9.4 169.1 %all-gather.18.cloned.1.call-start = ((), (), s32[]{:S(2)}) async-start(), calls=%async_computation.7 | async-start | bytes 8912896 | tf_op jit(solution)/shard_map/all_gather | solution.py:124
  10.1 259.7 %all-gather.20.cloned.1.call-start = ((), (), s32[]{:S(2)}) async-start(), calls=%async_computation.8 | async-start | bytes 8912896 | tf_op jit(solution)/shard_map/all_gather | solution.py:124
  10.9 293.0 %all-gather.10.cloned.1.call-start = ((), (), s32[]{:S(2)}) async-start(), calls=%async_computation.3 | async-start | bytes 3932160 | tf_op jit(solution)/shard_map/all_gather | solution.py:129
  87.2 3.4 copy-start.2
  134.5 193.5 %all-gather.12.cloned.1.call-start = ((), (), s32[]{:S(2)}) async-start(), calls=%async_computation.4 | async-start | bytes 3932160 | tf_op jit(solution)/shard_map/all_gather | solution.py:129
  178.5 3.4 copy-start.1
  225.8 132.2 %all-gather.14.cloned.1.call-start = ((), (), s32[]{:S(2)}) async-start(), calls=%async_computation.5 | async-start | bytes 3932160 | tf_op jit(solution)/shard_map/all_gather | solution.py:129
  269.8 3.4 copy-start
  273.2 30.4 %copy-start.9 = (s32[8,2]{0,1:T(2,128)S(1)}, s32[8,2]{0,1:T(2,128)}, u32[]{:S(2)}) copy-start(s32[8,2]{0,1:T(2,128)} %param.11) | copy-start | bytes 196
  273.2 30.4 %copy-start.8 = (f32[256]{0:T(256)S(1)}, f32[256]{0:T(256)}, u32[]{:S(2)}) copy-start(f32[256]{0:T(256)} %param.13) | copy-start | bytes 3076
  273.2 30.7 %copy-start.10 = (f32[2]{0:T(128)S(1)}, f32[2]{0:T(128)}, u32[]{:S(2)}) copy-start(f32[2]{0:T(128)} %param.15) | copy-start | bytes 28
  303.9 2.0 copy-start.4
  328.0 1.9 copy-start.5
  358.0 1.9 copy-start.6
Sparse Core Ops, SparseCore 0:
  9.5 77.5 all-gather.15
  89.3 89.1 all-gather.17
  180.6 89.1 all-gather.19
  271.2 26.7 all-gather.9
  299.4 28.5 all-gather.11
  329.4 28.5 all-gather.13

commit v2 on v0

v2 whole, which is shorter than its diff:
```python
import functools

import jax
import jax.numpy as jnp
from jax import lax
from jax.experimental import pallas as pl
from jax.experimental.pallas import tpu as pltpu
from jax.sharding import PartitionSpec as P

laplace_points = (0.06, 0.25, 0.7, 1.6, 3.5)
laplace_weights = (0.16, 0.36, 0.62, 1.0, 1.7)
lanes = 128


def tiles_kernel(slots_ref, coefficient_ref, center_ref, out_ref):
    out_ref[0] = lax.dot_general(
        center_ref[...],
        coefficient_ref[0],
        (((1,), (1,)), ((), ())),
        preferred_element_type=jnp.float32,
    ).astype(jnp.bfloat16)


def integral_tiles(coefficients, center, slot_tiles):
    slots, width, aux = coefficients.shape
    columns = center.shape[0]
    return pl.pallas_call(
        tiles_kernel,
        out_shape=jax.ShapeDtypeStruct((slots, columns, width), jnp.bfloat16),
        grid_spec=pltpu.PrefetchScalarGridSpec(
            num_scalar_prefetch=1,
            grid=(slots,),
            in_specs=[
                pl.BlockSpec((1, width, aux), lambda s, t: (t[s], 0, 0)),
                pl.BlockSpec((columns, aux), lambda s, t: (0, 0)),
            ],
            out_specs=pl.BlockSpec((1, columns, width), lambda s, t: (s, 0, 0)),
        ),
        compiler_params=pltpu.CompilerParams(vmem_limit_bytes=56 * 2**20),
        cost_estimate=pl.CostEstimate(
            flops=2 * slots * columns * width * aux,
            bytes_accessed=2 * (slots * width * aux + columns * aux + slots * columns * width),
            transcendentals=0,
        ),
    )(slot_tiles, coefficients, center)


def spread_kernel(
    left_count, right_count, right_rows, tiles_ref, amps_hbm, out_ref, amps_ref, held, total, part, sums,
    amps_sem, own_sem, send_slot, recv_slot, send_far, recv_far, send_near, recv_near, send_sum, recv_sum,
):
    slots = left_count * right_count
    ia, ib, op = lax.axis_index("ia"), lax.axis_index("ib"), lax.axis_index("op")
    me = ia * right_count + ib
    near = (op // 2) * 2 + 1 - op % 2
    far = (op + 2) % 4
    diagonal = (near + 2) % 4
    pairs, width, _ = amps_ref.shape
    share = tiles_ref.shape[1] // right_rows
    depth = 4 * share
    parts = width // lanes
    columns = slots // right_count * right_rows * lanes
    mesh_ids = pl.DeviceIdType.MESH

    def slot_device(s):
        return (s // right_count, s % right_count, op)

    near_device, far_device = (ia, ib, near), (ia, ib, far)

    load = pltpu.make_async_copy(amps_hbm, amps_ref, amps_sem)
    load.start()
    own = pltpu.make_async_copy(tiles_ref.at[me], held.at[op, me], own_sem)
    own.start()

    barrier = pltpu.get_barrier_semaphore()
    for k in range(1, slots):
        pl.semaphore_signal(
            barrier, inc=1, device_id=slot_device((me + k) % slots), device_id_type=mesh_ids
        )
    for device in (near_device, far_device):
        pl.semaphore_signal(barrier, inc=1, device_id=device, device_id_type=mesh_ids)
    pl.semaphore_wait(barrier, slots + 1)

    def to_slot(k):
        target = (me + k) % slots
        return pltpu.make_async_remote_copy(
            src_ref=tiles_ref.at[target], dst_ref=held.at[op, me],
            send_sem=send_slot.at[k], recv_sem=recv_slot.at[k],
            device_id=slot_device(target), device_id_type=mesh_ids,
        )

    def from_slot(k):
        source = (me + slots - k) % slots
        return pltpu.make_async_remote_copy(
            src_ref=tiles_ref.at[source], dst_ref=held.at[op, source],
            send_sem=send_slot.at[k], recv_sem=recv_slot.at[k],
            device_id=slot_device(source), device_id_type=mesh_ids,
        )

    def across(k, row, sends, receives, at, device):
        source = (me + slots - k) % slots
        return pltpu.make_async_remote_copy(
            src_ref=held.at[row, source], dst_ref=held.at[row, source],
            send_sem=sends.at[at], recv_sem=receives.at[at],
            device_id=device, device_id_type=mesh_ids,
        )

    for o in range(right_count):
        for a in range(left_count):
            if o + a > 0:
                to_slot(o + a * right_count).start()
    total[...] = jnp.zeros_like(total)
    own.wait()

    def contract(o):
        for a in range(left_count):
            k = o + a * right_count
            across(k, near, send_near, recv_near, k, near_device).wait_recv()
            across(k, diagonal, send_near, recv_near, slots + k, near_device).wait_recv()
        block = (ib + right_count - o) % right_count

        def one(j, carry):
            across_c = pl.ds(pl.multiple_of(j * lanes, lanes), lanes)
            left = amps_ref[
                :, across_c, pl.ds(pl.multiple_of(block * depth, lanes), depth)
            ].reshape(pairs * lanes, depth)
            right = jnp.concatenate(
                [
                    jnp.concatenate(
                        [
                            held[g, a * right_count + block, b * share : (b + 1) * share, across_c]
                            for g in range(4)
                        ],
                        axis=0,
                    )
                    for a in range(left_count)
                    for b in range(right_rows)
                ],
                axis=1,
            )
            total[...] += jnp.dot(left, right, preferred_element_type=jnp.float32)
            return carry

        lax.fori_loop(0, parts, one, 0)

    def step(o, carry):
        @pl.when(o < right_count)
        def _():
            for a in range(left_count):
                k = o + a * right_count

                @pl.when(k > 0)
                def _():
                    from_slot(k).wait_recv()

                across(k, op, send_far, recv_far, k, far_device).start()
                across(k, op, send_near, recv_near, k, near_device).start()
            for a in range(left_count):
                k = o + a * right_count
                across(k, far, send_far, recv_far, k, far_device).wait_recv()
                across(k, far, send_near, recv_near, slots + k, near_device).start()

        @pl.when(o == 0)
        def _():
            load.wait()

        @pl.when(o > 0)
        def _():
            contract(o - 1)

        return carry

    lax.fori_loop(0, right_count + 1, step, 0)

    row = lax.broadcasted_iota(jnp.int32, (lanes, columns), 0)
    column = lax.broadcasted_iota(jnp.int32, (lanes, columns), 1) % lanes
    for p in range(pairs):
        block = total[p * lanes : (p + 1) * lanes, :]
        part[p : p + 1, :] = jnp.sum(jnp.where(row == column, block, 0.0), axis=0, keepdims=True)

    def to_sum(k):
        return pltpu.make_async_remote_copy(
            src_ref=part, dst_ref=sums.at[k],
            send_sem=send_sum.at[k], recv_sem=recv_sum.at[k],
            device_id=slot_device((me + k) % slots), device_id_type=mesh_ids,
        )

    for k in range(1, slots):
        to_sum(k).start()
    for k in range(slots):
        if k > 0:
            to_slot(k).wait_send()
        across(k, op, send_far, recv_far, k, far_device).wait_send()
        across(k, op, send_near, recv_near, k, near_device).wait_send()
        across(k, far, send_near, recv_near, slots + k, near_device).wait_send()
    value = part[...]
    for k in range(1, slots):
        to_sum(k).wait_recv()
        value = value + sums[k]
    for k in range(1, slots):
        to_sum(k).wait_send()
    out_ref[...] = value


def spread_and_contract(tiles, amplitudes, right_rows):
    slots, rows, width = tiles.shape
    pairs, _, full = amplitudes.shape
    left_count, right_count = lax.axis_size("ia"), lax.axis_size("ib")
    columns = left_count * right_rows * lanes
    dma = pltpu.SemaphoreType.DMA
    return pl.pallas_call(
        functools.partial(spread_kernel, left_count, right_count, right_rows),
        out_shape=jax.ShapeDtypeStruct((pairs, columns), jnp.float32),
        in_specs=[pl.BlockSpec(memory_space=pltpu.VMEM), pl.BlockSpec(memory_space=pl.ANY)],
        out_specs=pl.BlockSpec(memory_space=pltpu.VMEM),
        scratch_shapes=[
            pltpu.VMEM((pairs, width, full), jnp.bfloat16),
            pltpu.VMEM((4, slots, rows, width), jnp.bfloat16),
            pltpu.VMEM((pairs * lanes, columns), jnp.float32),
            pltpu.VMEM((pairs, columns), jnp.float32),
            pltpu.VMEM((slots, pairs, columns), jnp.float32),
            dma, dma,
            dma((slots,)), dma((slots,)), dma((slots,)), dma((slots,)),
            dma((2 * slots,)), dma((2 * slots,)), dma((slots,)), dma((slots,)),
        ],
        compiler_params=pltpu.CompilerParams(
            collective_id=0, has_side_effects=True, vmem_limit_bytes=56 * 2**20
        ),
        cost_estimate=pl.CostEstimate(
            flops=2 * pairs * lanes * columns * full * (width // lanes),
            bytes_accessed=2 * (pairs * width * full + tiles.size),
            transcendentals=0,
        ),
    )(tiles, amplitudes)


def fused(fit_coefficients, three_center, amplitudes, slot_tiles):
    _, own_rows, aux = fit_coefficients.shape
    right_rows, _, share = three_center.shape
    local_pairs, tile_width, _ = amplitudes.shape
    slots = lax.axis_size("ia") * lax.axis_size("ib")
    center = jnp.transpose(three_center, (0, 2, 1)).reshape(right_rows * share, aux)
    gathered = lax.all_gather(fit_coefficients[0], ("ib", "op"), axis=0, tiled=True)
    tiles = integral_tiles(gathered.reshape(slots, tile_width, aux), center, slot_tiles)
    value = spread_and_contract(tiles, amplitudes, right_rows)
    return value.reshape(local_pairs, lax.axis_size("ia"), right_rows, lanes).sum(axis=3)


def whole_at_once(fit_coefficients, three_center, amplitudes, slot_tiles):
    left_rows = fit_coefficients.shape[0]
    right_rows = three_center.shape[0]
    share = three_center.shape[2]
    tile_width = amplitudes.shape[1]
    local_pairs = amplitudes.shape[0]
    left_count, right_count = lax.axis_size("ia"), lax.axis_size("ib")
    group_count = lax.axis_size("op")
    slot_count = left_count * right_count
    tiles = jnp.einsum(
        "oiu,tup->otip",
        lax.all_gather(fit_coefficients, ("ib", "op"), axis=1, tiled=True),
        three_center,
        preferred_element_type=jnp.float32,
    ).astype(jnp.bfloat16)
    tiles = tiles.reshape(left_rows, right_rows, slot_count, tile_width, share)
    ordered = jnp.concatenate(
        [lax.dynamic_slice_in_dim(tiles, slot_tiles[s], 1, axis=2) for s in range(slot_count)],
        axis=2,
    )
    arrived = lax.all_to_all(ordered, ("ia", "ib"), split_axis=2, concat_axis=0, tiled=True)
    received = arrived.reshape(left_count, right_count, left_rows, right_rows, tile_width, share)
    split_amps = amplitudes.reshape(local_pairs, tile_width, right_count, group_count * share)
    value = jnp.einsum(
        "pkie,aiobke->paob",
        split_amps,
        lax.all_gather(received, "op", axis=5, tiled=True),
        preferred_element_type=jnp.float32,
    )
    return value.reshape(local_pairs, left_count * left_rows, right_rows)


def per_device(
    fit_coefficients,
    three_center,
    amplitudes,
    pair_list,
    slot_tiles,
    energy_occupied,
    energy_left,
    energy_right,
):
    left_rows, own_rows, _ = fit_coefficients.shape
    right_rows, _, share = three_center.shape
    local_pairs, tile_width, _ = amplitudes.shape
    arguments = (fit_coefficients, three_center, amplitudes, slot_tiles)
    fits = (
        left_rows == 1
        and lax.axis_size("op") == 4
        and tile_width % lanes == 0
        and (4 * share) % lanes == 0
        and share % 16 == 0
        and local_pairs % 8 == 0
    )
    if fits:
        summed = fused(*arguments)
    else:
        summed = lax.psum(whole_at_once(*arguments), ("ia", "ib"))
    owned = lax.dynamic_slice(
        summed,
        (0, lax.axis_index("ia") * left_rows, 0),
        (local_pairs, left_rows, right_rows),
    )
    occupied = energy_occupied.shape[0]
    column = lax.broadcasted_iota(jnp.int32, (local_pairs, occupied), 1)
    occupied_one = jnp.sum(
        jnp.where(pair_list[:, 0:1] == column, energy_occupied[None, :], 0.0), axis=1
    )
    occupied_two = jnp.sum(
        jnp.where(pair_list[:, 1:2] == column, energy_occupied[None, :], 0.0), axis=1
    )
    occupied_sum = occupied_one + occupied_two
    denominator = (
        energy_left[None, :, None] + energy_right[None, None, :] - occupied_sum[:, None, None]
    )
    factor = jnp.zeros_like(denominator)
    for point, weight in zip(laplace_points, laplace_weights):
        factor = factor + weight * jnp.exp(-point * denominator)
    return owned * factor


def solution(mesh):
    placed = (
        P("ia", ("ib", "op"), None),
        P(None, None, ("ib", "op")),
        P("op", ("ia", "ib"), None),
        P("op", None),
        P(),
        P(),
        P("ia"),
        P(),
    )
    return jax.shard_map(
        per_device, mesh=mesh, in_specs=placed, out_specs=P("op", "ia", None), check_vma=False
    )
```

time: 359 us -> 263 us (0.73)
  Pallas kernels: 0 us -> 114 us
  blocking collectives: 77.8 us -> 0 us
  local copies, waits for them, and re-layouts: 77.7 us -> 0.76 us
  matrix products: 52.9 us -> 0 us
    pallas_call x0 -> x2, Pallas kernels: none -> 114 us  [the longest x1 94.5 us: spread_and_contract(): pl.pallas_call(functools.partial(spread_kernel, left_count, right_count,...]
    reshape x4 -> x0, local copies, waits for them, and re-layouts: 72.7 us -> none  [the longest x2 67.7 us: per_device(): amplitudes.reshape(local_pairs, tile_width, right_count, group_count * sh...]
    all_to_all x1 -> x0, blocking collectives: 60.4 us -> none  [per_device(): lax.all_to_all(ordered, ('ia', 'ib'), split_axis=2, concat_axis=0, tiled=...]
    dot_general x2 -> x0, matrix products: 52.9 us -> none  [the longest x1 37.6 us: per_device(): jnp.einsum('pkie,aibke->pab', split_amps, lax.all_gather(received, 'op',...]
    psum x1 -> x0, blocking collectives: 17.4 us -> none  [per_device(): summed = lax.psum(partial_value, ('ia', 'ib'))]
    all_gather x2 -> x1, waiting for transfers between devices: 131 us -> 130 us  [fused(): lax.all_gather(fit_coefficients[0], ('ib', 'op'), axis=0, tiled=True)]
  transfers between devices with their start and end apart: 2 -> 1, of which waited for: 1 -> 1; matrix products, arithmetic and copies ran while one was open for 19% -> 1% of each run, Pallas kernels for 0% -> 0%
where the time goes in v2:
time: 263 us
  waiting for transfers between devices  131 us (50%)
  Pallas kernels  114 us (43%)
  between operations  14.1 us (5%)
  other arithmetic  3.01 us (1%)
    all_gather x1, waiting for transfers between devices, fused(): lax.all_gather(fit_coefficients[0], ('ib', 'op'), axis=0, tiled=True)  130 us
    pallas_call x1, Pallas kernels, spread_and_contract(): pl.pallas_call(functools.partial(spread_kernel, left_count, right_count,...  94.5 us
    pallas_call x1, Pallas kernels, integral_tiles(): pl.pallas_call(tiles_kernel, out_shape=jax.ShapeDtypeStruct((slots, colum...  19.5 us
  transfers between devices with their start and end apart: 1, of which 1 were waited for; matrix products, arithmetic and copies ran while one was open for 1% of the time, Pallas kernels for 0%

profile of v2, /device:TPU:0, one launch (start us, length us, event | category | flops | bytes accessed | tf_op | source)
XLA Modules:
  0.0 262.5 jit_solution(17459328310799368913)
XLA Ops:
  6.5 0.0 all-gather.3.cloned.1.call-start
  6.5 0.7 all-gather.3.cloned.1.call-update
  7.9 0.8 slice_bitcast_fusion.1
  8.7 0.9 select_reduce_fusion
  9.6 0.7 broadcast_add_fusion
  10.2 130.0 %all-gather.3.cloned.1.call-done = bf16[1,3072,4096]{2,1,0:T(8,128)(2,1)} async-done(((bf16[1,192,4096]{2,1,0:T(8,128)(2,1)}), bf16[1,3072,4096]{2,1,0:T(8,128)(2,1)}) %all-gather.3.cloned.1.call-update) | async-done | bytes 25165840 | tf_op jit(solution)/shard_map/all_gather | solution.py:243
  140.3 19.5 %shard_map.82.tiles_ref = bf16[8,384,384]{2,1,0:T(8,128)(2,1)} custom-call(s32[8]{0:T(128)} %slots_ref.1, bf16[8,384,4096]{2,1,0:T(8,128)(2,1)} %bitcast.12, bf16[384,4096]{1,0:T(8,128)(2,1)} %bitcast.13), custom_call_target="tpu_custom_call" | custom-call | flops 9663676416 | bytes 30670848 | tf_op jit(solution)/shard_map/pallas_call | solution.py:27
  159.8 94.5 %shard_map.83 = f32[8,512]{1,0:T(8,128)} custom-call(bf16[8,384,384]{2,1,0:T(8,128)(2,1)} %shard_map.82.tiles_ref, bf16[8,384,3072]{2,1,0:T(8,128)(2,1)} %amps_hbm.1), custom_call_target="tpu_custom_call" | custom-call | flops 9663676416 | bytes 21233664 | tf_op jit(solution)/shard_map/pallas_call | solution.py:211
  254.2 0.8 reduce_sum.27
  255.0 0.6 fusion.10
  (1 shorter events, 0.0 us)
Async XLA Ops:
  6.5 133.7 %all-gather.3.cloned.1.call-start = ((), (), s32[]{:S(2)}) async-start(), calls=%async_computation | async-start | bytes 26738688 | tf_op jit(solution)/shard_map/all_gather | solution.py:243
Sparse Core Ops, SparseCore 0:
  9.0 131.2 all-gather.2

commit v3 on v2

--- a/solution.py
+++ b/solution.py
@@ -12,13 +12,14 @@
 lanes = 128
 
 
-def tiles_kernel(slots_ref, coefficient_ref, center_ref, out_ref):
-    out_ref[0] = lax.dot_general(
-        center_ref[...],
-        coefficient_ref[0],
-        (((1,), (1,)), ((), ())),
-        preferred_element_type=jnp.float32,
+def tiles_kernel(slots_ref, first_ref, second_ref, center_ref, out_ref):
+    rows = jnp.concatenate([first_ref[0], second_ref[0]], axis=0)
+    width = first_ref.shape[1]
+    product = lax.dot_general(
+        center_ref[...], rows, (((1,), (1,)), ((), ())), preferred_element_type=jnp.float32
     ).astype(jnp.bfloat16)
+    out_ref[0] = product[:, :width]
+    out_ref[1] = product[:, width:]
 
 
 def integral_tiles(coefficients, center, slot_tiles):
@@ -29,12 +30,13 @@
         out_shape=jax.ShapeDtypeStruct((slots, columns, width), jnp.bfloat16),
         grid_spec=pltpu.PrefetchScalarGridSpec(
             num_scalar_prefetch=1,
-            grid=(slots,),
+            grid=(slots // 2,),
             in_specs=[
-                pl.BlockSpec((1, width, aux), lambda s, t: (t[s], 0, 0)),
+                pl.BlockSpec((1, width, aux), lambda s, t: (t[2 * s], 0, 0)),
+                pl.BlockSpec((1, width, aux), lambda s, t: (t[2 * s + 1], 0, 0)),
                 pl.BlockSpec((columns, aux), lambda s, t: (0, 0)),
             ],
-            out_specs=pl.BlockSpec((1, columns, width), lambda s, t: (s, 0, 0)),
+            out_specs=pl.BlockSpec((2, columns, width), lambda s, t: (s, 0, 0)),
         ),
         compiler_params=pltpu.CompilerParams(vmem_limit_bytes=56 * 2**20),
         cost_estimate=pl.CostEstimate(
@@ -42,7 +44,7 @@
             bytes_accessed=2 * (slots * width * aux + columns * aux + slots * columns * width),
             transcendentals=0,
         ),
-    )(slot_tiles, coefficients, center)
+    )(slot_tiles, coefficients, coefficients, center)
 
 
 def spread_kernel(
@@ -295,6 +297,7 @@
     fits = (
         left_rows == 1
         and lax.axis_size("op") == 4
+        and (lax.axis_size("ia") * lax.axis_size("ib")) % 2 == 0
         and tile_width % lanes == 0
         and (4 * share) % lanes == 0
         and share % 16 == 0

time: 263 us -> 260 us (0.989)
  Pallas kernels: 114 us -> 111 us
    pallas_call x1, Pallas kernels: 19.5 us -> 16.3 us  [integral_tiles(): pl.pallas_call(tiles_kernel, out_shape=jax.ShapeDtypeStruct((slots, colum...]
where the time goes in v3:
time: 260 us; the launch traced here: 259 us
  waiting for transfers between devices  131 us (50%)
  Pallas kernels  111 us (43%)
  between operations  14.1 us (5%)
  other arithmetic  3.01 us (1%)
    all_gather x1, waiting for transfers between devices, fused(): lax.all_gather(fit_coefficients[0], ('ib', 'op'), axis=0, tiled=True)  130 us
    pallas_call x1, Pallas kernels, spread_and_contract(): pl.pallas_call(functools.partial(spread_kernel, left_count, right_count,...  94.5 us
    pallas_call x1, Pallas kernels, integral_tiles(): pl.pallas_call(tiles_kernel, out_shape=jax.ShapeDtypeStruct((slots, colum...  16.3 us
  transfers between devices with their start and end apart: 1, of which 1 were waited for; matrix products, arithmetic and copies ran while one was open for 1% of the time, Pallas kernels for 0%

profile of v3, /device:TPU:0, one launch (start us, length us, event | category | flops | bytes accessed | tf_op | source)
XLA Modules:
  0.0 259.4 jit_solution(3972392855075464200)
XLA Ops:
  6.5 0.0 all-gather.3.cloned.1.call-start
  6.5 0.7 all-gather.3.cloned.1.call-update
  7.9 0.8 slice_bitcast_fusion.1
  8.7 0.9 select_reduce_fusion
  9.6 0.7 broadcast_add_fusion
  10.2 130.0 %all-gather.3.cloned.1.call-done = bf16[1,3072,4096]{2,1,0:T(8,128)(2,1)} async-done(((bf16[1,192,4096]{2,1,0:T(8,128)(2,1)}), bf16[1,3072,4096]{2,1,0:T(8,128)(2,1)}) %all-gather.3.cloned.1.call-update) | async-done | bytes 25165840 | tf_op jit(solution)/shard_map/all_gather | solution.py:245
  140.3 16.3 %shard_map.82.tiles_ref = bf16[8,384,384]{2,1,0:T(8,128)(2,1)} custom-call(s32[8]{0:T(128)} %slots_ref.1, bf16[8,384,4096]{2,1,0:T(8,128)(2,1)} %bitcast.11, bf16[8,384,4096]{2,1,0:T(8,128)(2,1)} %bitcast.12, bf16[384,4096]{1,0:T(8,128)(2,1)} %bitcast.13), custom_call_target="tpu_custom_call" | custom-call | flops 9663676416 | bytes 30670848 | tf_op jit(solution)/shard_map/pallas_call | solution.py:28
  156.6 94.5 %shard_map.83 = f32[8,512]{1,0:T(8,128)} custom-call(bf16[8,384,384]{2,1,0:T(8,128)(2,1)} %shard_map.82.tiles_ref, bf16[8,384,3072]{2,1,0:T(8,128)(2,1)} %amps_hbm.1), custom_call_target="tpu_custom_call" | custom-call | flops 9663676416 | bytes 21233664 | tf_op jit(solution)/shard_map/pallas_call | solution.py:213
  251.1 0.8 reduce_sum.27
  251.9 0.6 fusion.10
  (1 shorter events, 0.0 us)
Async XLA Ops:
  6.5 133.7 %all-gather.3.cloned.1.call-start = ((), (), s32[]{:S(2)}) async-start(), calls=%async_computation | async-start | bytes 26738688 | tf_op jit(solution)/shard_map/all_gather | solution.py:245
Sparse Core Ops, SparseCore 0:
  9.0 131.2 all-gather.2
